TPU v7x, 32 devices: a whole 2x2x4 slice. The times are simulated.
32 devices in a mesh: parts: 2 (over x), adapt: 16 (over z, y, core).
Axes of the slice: x: 2, y: 2, z: 4, core: 2. Of those that a mesh axis runs over, the one named last changes fastest.
Arguments:
- hidden_norm_rows: bfloat16 [256, 8192], P(('parts', 'adapt')), parts along dimension 0, may hold values from -6 to 6
- value_weight: bfloat16 [8192, 1024], P('adapt'), may hold values from -0.0625 to 0.0625
- adapter_down_weight: bfloat16 [96, 8192, 64], P('adapt'), may hold values from -0.0625 to 0.0625
- adapter_up_weight: bfloat16 [96, 64, 1024], P('adapt'), may hold values from -0.75 to 0.75
- adapter_per_block: int32 [2], P('parts'), parts along dimension 0, may hold values from 0 to 95
- block_live_rows: int32 [2], P('parts'), parts along dimension 0, may hold values from 1 to 128
- queries: bfloat16 [256, 8192], P(('parts', 'adapt')), parts along dimension 0, may hold values from -100 to 100
- incoming_key: bfloat16 [256, 1024], P(('parts', 'adapt')), parts along dimension 0, may hold values from -6 to 6
- key_cache: bfloat16 [256, 32, 1024], P(('parts', 'adapt')), parts along dimension 0, may hold values from -4 to 4
- value_cache: bfloat16 [256, 32, 1024], P(('parts', 'adapt')), parts along dimension 0, may hold values from -6 to 6
- cache_length: int32 [256], P(('parts', 'adapt')), parts along dimension 0, may hold values from 2 to 32
Outputs:
- new_value: bfloat16 [256, 1024], P(('parts', 'adapt')), parts along dimension 0
- attended: bfloat16 [256, 8192], P(('parts', 'adapt')), parts along dimension 0
There are 2 independent parts, one for each index of `parts`. A program takes and returns all parts, laid end to end along the dimension named above; an argument that names none is the same for every part. Nothing has to cross between parts.
All inputs are finite; a program needn't handle non-finite values.
Results may differ from a plain program's by a relative error of at most 0.007.
Values may be sent and summed in bfloat16 or wider, within the bound.
A program may use at most 128 MiB of HBM per device.

v0:
```python
import jax
import jax.numpy as jnp
from jax import lax
from jax.sharding import PartitionSpec as P

HEADS = 64
KV_HEADS = 8
HD = 128
BLOCK_ROWS = 128


def broadcast(value, axis, source):
    kept = jnp.where(lax.axis_index(axis) == source, value, 0).astype(value.dtype)
    return lax.psum(kept, axis)


def on_device(
    hidden_norm_rows,
    value_weight,
    adapter_down_weight,
    adapter_up_weight,
    adapter_per_block,
    block_live_rows,
    queries,
    incoming_key,
    key_cache,
    value_cache,
    cache_length,
):
    rows_dev = hidden_norm_rows.shape[0]
    resident_count = adapter_down_weight.shape[0]
    cached = key_cache.shape[1]
    group = HEADS // KV_HEADS
    scale = HD ** (-0.5)
    first_row = lax.axis_index("adapt") * rows_dev
    local_rows = first_row + jnp.arange(rows_dev, dtype=jnp.int32)
    my_block = first_row // BLOCK_ROWS
    live = (local_rows % BLOCK_ROWS < block_live_rows[local_rows // BLOCK_ROWS]).astype(
        jnp.float32
    )[:, None]
    query = queries.reshape(rows_dev, KV_HEADS, group, HD)
    keys = key_cache.reshape(rows_dev, cached, KV_HEADS, HD)
    scores = jnp.einsum("rgqd,rpgd->rgqp", query, keys, preferred_element_type=jnp.float32) * scale
    valid = jnp.arange(cached, dtype=jnp.int32)[None, :] < cache_length[:, None]
    scores = jnp.where(valid[:, None, None, :], scores, -1e30)
    fresh = incoming_key.reshape(rows_dev, KV_HEADS, HD)
    score_new = (
        jnp.einsum("rgqd,rgd->rgq", query, fresh, preferred_element_type=jnp.float32) * scale
    )
    top = jnp.maximum(jnp.max(scores, axis=-1), score_new)
    expo = jnp.exp(scores - top[..., None])
    expo_new = jnp.exp(score_new - top)
    total = jnp.sum(expo, axis=-1) + expo_new
    weights = (expo / total[..., None]).astype(jnp.bfloat16)
    weight_new = (expo_new / total).astype(jnp.bfloat16)
    values = value_cache.reshape(rows_dev, cached, KV_HEADS, HD)
    cached_mix = jnp.einsum("rgqp,rpgd->rgqd", weights, values, preferred_element_type=jnp.float32)
    spread = lax.all_to_all(hidden_norm_rows, "adapt", split_axis=1, concat_axis=0, tiled=True)
    base = lax.psum_scatter(
        jnp.dot(spread, value_weight, preferred_element_type=jnp.float32),
        "adapt",
        scatter_dimension=0,
        tiled=True,
    )

    def fetch_step(block, held):
        wanted = adapter_per_block[block]
        owner = wanted // resident_count
        adapter_position = wanted % resident_count
        offered_down = lax.dynamic_index_in_dim(
            adapter_down_weight, adapter_position, 0, keepdims=False
        )
        offered_up = lax.dynamic_index_in_dim(
            adapter_up_weight, adapter_position, 0, keepdims=False
        )
        got_a, got_b = (
            broadcast(offered_down, "adapt", owner),
            broadcast(offered_up, "adapt", owner),
        )
        take = block == my_block
        return (jnp.where(take, got_a, held[0]), jnp.where(take, got_b, held[1]))

    start_pair = (
        jnp.zeros(adapter_down_weight.shape[1:], jnp.bfloat16),
        jnp.zeros(adapter_up_weight.shape[1:], jnp.bfloat16),
    )
    down_map, up_map = lax.fori_loop(0, adapter_per_block.shape[0], fetch_step, start_pair)
    reduced_rank_state = jnp.dot(
        hidden_norm_rows, down_map, preferred_element_type=jnp.float32
    ).astype(jnp.bfloat16)
    delta = jnp.dot(reduced_rank_state, up_map, preferred_element_type=jnp.float32)
    new_value = (live * (base + delta)).astype(jnp.bfloat16)
    own_value = new_value.reshape(rows_dev, KV_HEADS, 1, HD).astype(jnp.float32)
    mixed = cached_mix + weight_new.astype(jnp.float32)[..., None] * own_value
    attended = (live * mixed.reshape(rows_dev, HEADS * HD)).astype(jnp.bfloat16)
    return (new_value, attended)


def solution(mesh):
    return jax.shard_map(
        on_device,
        mesh=mesh,
        in_specs=(
            P(("parts", "adapt"), None),
            P("adapt", None),
            P("adapt", None, None),
            P("adapt", None, None),
            P("parts"),
            P("parts"),
            P(("parts", "adapt"), None),
            P(("parts", "adapt"), None),
            P(("parts", "adapt"), None, None),
            P(("parts", "adapt"), None, None),
            P(("parts", "adapt")),
        ),
        out_specs=(P(("parts", "adapt"), None), P(("parts", "adapt"), None)),
        check_vma=False,
    )
```

profile of v0, /device:TPU:0, one launch (start us, length us, event | category | flops | bytes accessed | tf_op | source)
XLA Modules:
  0.0 183.6 jit_solution(11682047590291873048)
XLA Ops:
  7.2 0.0 copy-start
  7.2 0.0 copy-start.1
  7.2 0.0 copy-start.2
  7.2 0.0 copy-start.4
  7.2 0.0 copy-start.3
  7.2 7.5 %all-to-all-start = ((bf16[8,16,512]{2,0,1:T(8,128)(2,1)}), bf16[8,16,512]{2,0,1:T(8,128)(2,1)S(1)}, u32[]{:S(2)}, u32[]{:S(2)}) async-start(bf16[8,16,512]{2,0,1:T(8,128)(2,1)} %bitcast.51), calls=%async_computation | async-start | bytes 262144 | tf_op jit(solution)/shard_map/all_to_all | solution.py:58
  14.8 0.0 all-reduce.3.cloned.1.call-start
  15.5 2.3 %select_bitcast_fusion = bf16[8192,64]{0,1:T(8,128)(2,1)} fusion(bf16[6,8192,64]{1,2,0:T(8,128)(2,1)} %param.13, s32[]{:T(128)S(6)} %select_n.96, pred[]{:T(512)S(6)} %eq.15), kind=kLoop, calls=%fused_computation.9 | loop fusion | flops 524288 | bytes 2097157 | tf_op jit(solution)/shard_map/while/body/eval_jaxpr/jit(_where)/select_n | solution.py:13
  17.8 1.6 select_bitcast_fusion.1
  19.4 0.0 all-reduce.3.cloned.1.call-update
  19.4 0.0 reduce-scatter.2.cloned.1.call-start
  20.1 0.7 iota_compare_fusion
  20.9 1.6 fusion.34
  22.5 0.2 all-to-all-done
  22.7 0.0 copy-done
  22.7 1.1 fusion.16
  23.8 0.0 reduce-scatter.2.cloned.1.call-update
  23.8 0.0 copy-done.2
  23.8 0.0 copy-done.4
  23.9 0.2 fusion.22
  24.1 0.3 fusion.15
  24.4 90.4 %all-reduce.3.cloned.1.call-done = (bf16[8192,64]{0,1:T(8,128)(2,1)}, bf16[64,1024]{1,0:T(8,128)(2,1)}) async-done(((bf16[8192,64]{0,1:T(8,128)(2,1)}, bf16[64,1024]{1,0:T(8,128)(2,1)}), (bf16[8192,64]{0,1:T(8,128)(2,1)}, bf16[64,1024]{1,0:T(8,128)(2,1)})) %all-reduce.3.cloned.1.call-update) | async-done | bytes 1179664 | tf_op jit(solution)/shard_map/while/body/eval_jaxpr/psum | solution.py:14
  114.8 58.4 %reduce-scatter.2.cloned.1.call-done = f32[8,1024]{1,0:T(8,128)} async-done(((f32[128,1024]{1,0:T(8,128)}), f32[8,1024]{1,0:T(8,128)}) %reduce-scatter.2.cloned.1.call-update) | async-done | bytes 32784 | tf_op jit(solution)/shard_map/reduce_scatter | solution.py:59
  173.2 0.0 copy-done.1
  173.2 2.5 %bitcast_convert_fusion = (f32[8,8,128]{2,0,1:T(8,128)S(1)}, bf16[8,1024]{1,0:T(8,128)(2,1)}) fusion(f32[8,1024]{1,0:T(8,128)} %reduce-scatter.2.cloned.1.call-done, bf16[64,1024]{1,0:T(8,128)(2,1)} %get-tuple-element.19, pred[]{:T(512)S(6)} %eq.14, bf16[8,8192]{1,0:T(8,128)(2,1)S(1)} %copy-done.1, bf16[8192,64]{0,1:T(8,128)(2,1)} %get-tuple-element.18, ...), kind=kOutput, calls=%fused_computation.37 | convolution fusion | flops 10060288 | bytes 1392673 | tf_op jit(solution)/shard_map/dot_general | solution.py:91
  175.6 0.0 copy-done.3
  175.6 0.3 fusion
  176.0 0.8 fusion.14
  (4 shorter events, 0.0 us)
Async XLA Ops:
  7.2 15.5 %copy-start = (bf16[512,1024]{1,0:T(8,128)(2,1)S(1)}, bf16[512,1024]{1,0:T(8,128)(2,1)}, u32[]{:S(2)}) copy-start(bf16[512,1024]{1,0:T(8,128)(2,1)} %param.12) | copy-start | bytes 3145732
  7.2 166.0 %copy-start.1 = (bf16[8,8192]{1,0:T(8,128)(2,1)S(1)}, bf16[8,8192]{1,0:T(8,128)(2,1)}, u32[]{:S(2)}) copy-start(bf16[8,8192]{1,0:T(8,128)(2,1)} %param.11) | copy-start | bytes 393220
  7.2 16.6 %copy-start.2 = (bf16[8,8192]{1,0:T(8,128)(2,1)S(1)}, bf16[8,8192]{1,0:T(8,128)(2,1)}, u32[]{:S(2)}) copy-start(bf16[8,8192]{1,0:T(8,128)(2,1)} %param.17) | copy-start | bytes 393220
  7.2 16.6 %copy-start.4 = (bf16[8,1024]{1,0:T(8,128)(2,1)S(1)}, bf16[8,1024]{1,0:T(8,128)(2,1)}, u32[]{:S(2)}) copy-start(bf16[8,1024]{1,0:T(8,128)(2,1)} %param.18) | copy-start | bytes 49156
  7.2 168.4 %copy-start.3 = (bf16[8,32,1024]{2,1,0:T(8,128)(2,1)S(1)}, bf16[8,32,1024]{2,1,0:T(8,128)(2,1)}, u32[]{:S(2)}) copy-start(bf16[8,32,1024]{2,1,0:T(8,128)(2,1)} %param.20) | copy-start | bytes 1572868
  7.2 15.5 %all-to-all-start = ((bf16[8,16,512]{2,0,1:T(8,128)(2,1)}), bf16[8,16,512]{2,0,1:T(8,128)(2,1)S(1)}, u32[]{:S(2)}, u32[]{:S(2)}) async-start(bf16[8,16,512]{2,0,1:T(8,128)(2,1)} %bitcast.51), calls=%async_computation | async-start | bytes 262144 | tf_op jit(solution)/shard_map/all_to_all | solution.py:58
  14.8 100.0 %all-reduce.3.cloned.1.call-start = ((), (), s32[]{:S(2)}) async-start(), calls=%async_computation.3 | async-start | bytes 2359296 | tf_op jit(solution)/shard_map/while/body/eval_jaxpr/psum | solution.py:14
  19.4 153.7 %reduce-scatter.2.cloned.1.call-start = ((), (), s32[]{:S(2)}) async-start(), calls=%async_computation.2 | async-start | bytes 557056 | tf_op jit(solution)/shard_map/reduce_scatter | solution.py:59
Sparse Core Ops, SparseCore 0:
  19.7 95.1 all-reduce.2
  118.3 54.7 reduce-scatter.1
where the time goes:
time: 184 us
  waiting for transfers between devices  149 us (81%)
  between operations  15.5 us (8%)
  starting transfers between devices  7.61 us (4%)
  other arithmetic  5.75 us (3%)
  matrix products  5.68 us (3%)
    psum x1, waiting for transfers between devices, broadcast(): return lax.psum(kept, axis)  90.4 us
    reduce_scatter x1, waiting for transfers between devices, on_device(): lax.psum_scatter(jnp.dot(spread, value_weight, preferred_element_type=jnp...  58.4 us
    all_to_all x1, starting transfers between devices, on_device(): lax.all_to_all(hidden_norm_rows, 'adapt', split_axis=1, concat_axis=0, ti...  7.53 us
    select_n x2, other arithmetic, broadcast(): jnp.where(lax.axis_index(axis) == source, value, 0).astype(value.dtype)  3.91 us
  transfers between devices with their start and end apart: 3, of which 3 were waited for; matrix products, arithmetic and copies ran while one was open for 4% of the time, Pallas kernels for 0%

commit v1 on v0

v1 whole, which is shorter than its diff:
```python
import functools

import jax
import jax.numpy as jnp
from jax import lax
from jax.experimental import pallas as pl
from jax.experimental.pallas import tpu as pltpu
from jax.sharding import PartitionSpec as P

HEADS = 64
KV_HEADS = 8
HD = 128
BLOCK_ROWS = 128
GROUP = HEADS // KV_HEADS
PLANE = 4
NT = (((1,), (1,)), ((), ()))


def kernel(
    n,
    adapter_ref,
    live_ref,
    length_ref,
    hidden_ref,
    weight_hbm,
    down_hbm,
    up_hbm,
    query_hbm,
    fresh_hbm,
    key_hbm,
    value_hbm,
    new_value_ref,
    attended_ref,
    gathered,
    plane_rows,
    partial,
    landed,
    weight_v,
    down_v,
    up_v,
    query_v,
    fresh_v,
    key_v,
    value_v,
    mix_v,
    fresh_weight_v,
    local_sem,
    send_sem,
    recv_sem,
    sum_send_sem,
    sum_recv_sem,
):
    rows = hidden_ref.shape[0]
    features = weight_v.shape[0]
    resident = down_v.shape[0]
    cached = key_v.shape[1]
    planes = n // PLANE
    me = lax.axis_index("adapt")
    core = lax.rem(me, 2)
    column = lax.rem(lax.div(me, 2), 2)
    level = lax.div(me, PLANE)

    def at(z, y, c):
        return z * PLANE + y * 2 + c

    locals_ = [
        pltpu.make_async_copy(src, dst, local_sem.at[i])
        for i, (src, dst) in enumerate(
            [
                (query_hbm, query_v),
                (fresh_hbm, fresh_v),
                (key_hbm, key_v),
                (value_hbm, value_v),
                (hidden_ref, gathered.at[me]),
                (weight_hbm, weight_v),
                (up_hbm, up_v),
                (down_hbm, down_v),
            ]
        )
    ]
    for copy in locals_:
        copy.start()

    barrier = pltpu.get_barrier_semaphore()
    for k in range(1, n):
        pl.semaphore_signal(
            barrier,
            inc=1,
            device_id={"adapt": lax.rem(me + k, n)},
            device_id_type=pl.DeviceIdType.MESH,
        )
    pl.semaphore_wait(barrier, n - 1)

    sends = []

    def give(block, target, own=False):
        copy = pltpu.make_async_remote_copy(
            src_ref=hidden_ref if own else gathered.at[block],
            dst_ref=gathered.at[block],
            send_sem=send_sem.at[len(sends)],
            recv_sem=recv_sem.at[block],
            device_id={"adapt": target},
            device_id_type=pl.DeviceIdType.MESH,
        )
        copy.start()
        sends.append(copy)

    def take(block):
        pltpu.make_async_remote_copy(
            src_ref=gathered.at[block],
            dst_ref=gathered.at[block],
            send_sem=send_sem.at[0],
            recv_sem=recv_sem.at[block],
            device_id={"adapt": at(level, column, 1 - core)},
            device_id_type=pl.DeviceIdType.MESH,
        ).wait_recv()

    sibling = at(level, column, 1 - core)
    across = at(level, 1 - column, core)
    give(me, across, own=True)
    for k in range(1, planes):
        give(me, at(lax.rem(level + k, planes), column, core), own=True)
    give(me, sibling, own=True)

    sequence = lax.broadcasted_iota(jnp.int32, (rows * GROUP, 1), 0)
    row_of = lax.rem(sequence, rows)
    lengths = jnp.zeros((rows * GROUP, 1), jnp.int32)
    for r in range(rows):
        lengths = jnp.where(row_of == r, length_ref[r], lengths)
    position = lax.broadcasted_iota(jnp.int32, (rows * GROUP, rows * cached), 1)
    valid = (lax.div(position, cached) == row_of) & (lax.rem(position, cached) < lengths)
    scale = HD ** (-0.5)

    def attend(g):
        q = jnp.concatenate(
            [
                query_v[:, (g * GROUP + h) * HD : (g * GROUP + h + 1) * HD].astype(jnp.float32)
                for h in range(GROUP)
            ],
            axis=0,
        )
        keys = key_v[:, :, g * HD : (g + 1) * HD].reshape(rows * cached, HD)
        values = value_v[:, :, g * HD : (g + 1) * HD].reshape(rows * cached, HD)
        fresh = jnp.concatenate(
            [fresh_v[:, g * HD : (g + 1) * HD].astype(jnp.float32)] * GROUP, axis=0
        )
        scores = (
            lax.dot_general(q.astype(jnp.bfloat16), keys, NT, preferred_element_type=jnp.float32)
            * scale
        )
        scores = jnp.where(valid, scores, -1e30)
        score_new = jnp.sum(q * fresh, axis=1, keepdims=True) * scale
        top = jnp.maximum(jnp.max(scores, axis=1, keepdims=True), score_new)
        expo = jnp.exp(scores - top)
        expo_new = jnp.exp(score_new - top)
        inverse = 1.0 / (jnp.sum(expo, axis=1, keepdims=True) + expo_new)
        weights = (expo * inverse).astype(jnp.bfloat16)
        mix_v[g] = jnp.dot(weights, values, preferred_element_type=jnp.float32)
        fresh_weight_v[g] = jnp.broadcast_to(
            (expo_new * inverse).astype(jnp.bfloat16).astype(jnp.float32), (rows * GROUP, HD)
        )

    sum_sends = []

    def process(k):
        z = lax.rem(level + planes - k, planes)
        for y, c in ((column, 1 - core), (1 - column, 1 - core)):
            take(at(z, y, c))
        plane_rows[...] = jnp.concatenate(
            [gathered[z * PLANE + i].astype(jnp.float32) for i in range(PLANE)], axis=0
        ).astype(jnp.bfloat16)
        wanted = adapter_ref[lax.div(z * PLANE * rows, BLOCK_ROWS)] - me * resident
        held = (wanted >= 0) & (wanted < resident)
        wanted = jnp.clip(wanted, 0, resident - 1)
        state = lax.dot_general(
            plane_rows[...], down_v[wanted], NT, preferred_element_type=jnp.float32
        )
        columns = pl.ds(pl.multiple_of(me * features, features), features)
        base = jnp.dot(
            plane_rows[:, columns], weight_v[...], preferred_element_type=jnp.float32
        )
        delta = jnp.dot(
            state.astype(jnp.bfloat16), up_v[wanted], preferred_element_type=jnp.float32
        )
        share = base + jnp.where(held, delta, 0.0)
        for i in range(PLANE):
            partial[z * PLANE + i] = share[i * rows : (i + 1) * rows].astype(jnp.bfloat16)
        targets = [at(z, y, c) for y in (1 - column, column) for c in (core, 1 - core)]
        if k == 0:
            targets = [at(z, 1 - column, core), at(z, 1 - column, 1 - core), sibling]
        for target in targets:
            copy = pltpu.make_async_remote_copy(
                src_ref=partial.at[target],
                dst_ref=landed.at[me],
                send_sem=sum_send_sem.at[len(sum_sends)],
                recv_sem=sum_recv_sem.at[me],
                device_id={"adapt": target},
                device_id_type=pl.DeviceIdType.MESH,
            )
            copy.start()
            sum_sends.append(copy)

    for copy in locals_[:4]:
        copy.wait()
    attend(0)
    attend(1)
    take(across)
    give(across, sibling)
    attend(2)
    attend(3)
    for copy in locals_[4:]:
        copy.wait()
    todo = list(range(4, KV_HEADS))
    for k in range(1, planes):
        z = lax.rem(level + planes - k, planes)
        block = at(z, column, core)
        take(block)
        give(block, across)
        give(block, sibling)
        if k >= 2:
            before = at(lax.rem(level + planes - (k - 1), planes), 1 - column, core)
            take(before)
            give(before, sibling)
        process(k - 1)
        if todo:
            attend(todo.pop(0))
    last = at(lax.rem(level + 1, planes), 1 - column, core)
    if planes > 1:
        take(last)
        give(last, sibling)
    while todo:
        attend(todo.pop(0))
    process(planes - 1)

    total = partial[me].astype(jnp.float32)
    for k in range(1, n):
        source = lax.rem(me + k, n)
        pltpu.make_async_remote_copy(
            src_ref=partial.at[source],
            dst_ref=landed.at[source],
            send_sem=sum_send_sem.at[0],
            recv_sem=sum_recv_sem.at[source],
            device_id={"adapt": source},
            device_id_type=pl.DeviceIdType.MESH,
        ).wait_recv()
        total = total + landed[source].astype(jnp.float32)
    first = me * rows
    local = lax.rem(first, BLOCK_ROWS) + lax.broadcasted_iota(jnp.int32, (rows, 1), 0)
    live = (local < live_ref[lax.div(first, BLOCK_ROWS)]).astype(jnp.float32)
    new_value = (live * total).astype(jnp.bfloat16)
    new_value_ref[...] = new_value
    own = new_value.astype(jnp.float32)
    for g in range(KV_HEADS):
        own_group = own[:, g * HD : (g + 1) * HD]
        for h in range(GROUP):
            part = slice(h * rows, (h + 1) * rows)
            mixed = mix_v[g, part, :] + fresh_weight_v[g, part, :] * own_group
            head = g * GROUP + h
            attended_ref[:, head * HD : (head + 1) * HD] = (live * mixed).astype(jnp.bfloat16)
    for copy in sends + sum_sends:
        copy.wait_send()


def on_device(
    n,
    hidden_norm_rows,
    value_weight,
    adapter_down_weight,
    adapter_up_weight,
    adapter_per_block,
    block_live_rows,
    queries,
    incoming_key,
    key_cache,
    value_cache,
    cache_length,
):
    rows, width = hidden_norm_rows.shape
    down = jnp.swapaxes(adapter_down_weight, 1, 2)
    wide = value_weight.shape[1]
    planes = n // PLANE
    bf16 = jnp.bfloat16
    sends = 3 * (planes - 1) + 2 + planes
    smem = pl.BlockSpec(memory_space=pltpu.SMEM)
    anywhere = pl.BlockSpec(memory_space=pl.ANY)
    vmem = pl.BlockSpec(memory_space=pltpu.VMEM)
    return pl.pallas_call(
        functools.partial(kernel, n),
        out_shape=(
            jax.ShapeDtypeStruct((rows, wide), bf16),
            jax.ShapeDtypeStruct(queries.shape, bf16),
        ),
        in_specs=[smem] * 3 + [anywhere] * 8,
        out_specs=(vmem, vmem),
        scratch_shapes=[
            pltpu.VMEM((n, rows, width), bf16),
            pltpu.VMEM((PLANE * rows, width), bf16),
            pltpu.VMEM((n, rows, wide), bf16),
            pltpu.VMEM((n, rows, wide), bf16),
            pltpu.VMEM(value_weight.shape, bf16),
            pltpu.VMEM(down.shape, bf16),
            pltpu.VMEM(adapter_up_weight.shape, bf16),
            pltpu.VMEM(queries.shape, bf16),
            pltpu.VMEM(incoming_key.shape, bf16),
            pltpu.VMEM(key_cache.shape, bf16),
            pltpu.VMEM(value_cache.shape, bf16),
            pltpu.VMEM((KV_HEADS, GROUP * rows, HD), jnp.float32),
            pltpu.VMEM((KV_HEADS, GROUP * rows, HD), jnp.float32),
            pltpu.SemaphoreType.DMA((8,)),
            pltpu.SemaphoreType.DMA((sends,)),
            pltpu.SemaphoreType.DMA((n,)),
            pltpu.SemaphoreType.DMA((n,)),
            pltpu.SemaphoreType.DMA((n,)),
        ],
        compiler_params=pltpu.CompilerParams(
            collective_id=0, has_side_effects=True, vmem_limit_bytes=48 * 1024 * 1024
        ),
    )(
        adapter_per_block,
        block_live_rows,
        cache_length,
        hidden_norm_rows,
        value_weight,
        down,
        adapter_up_weight,
        queries,
        incoming_key,
        key_cache,
        value_cache,
    )


def solution(mesh):
    return jax.shard_map(
        functools.partial(on_device, mesh.shape["adapt"]),
        mesh=mesh,
        in_specs=(
            P(("parts", "adapt"), None),
            P("adapt", None),
            P("adapt", None, None),
            P("adapt", None, None),
            P("parts"),
            P("parts"),
            P(("parts", "adapt"), None),
            P(("parts", "adapt"), None),
            P(("parts", "adapt"), None, None),
            P(("parts", "adapt"), None, None),
            P(("parts", "adapt")),
        ),
        out_specs=(P(("parts", "adapt"), None), P(("parts", "adapt"), None)),
        check_vma=False,
    )
```

time: 184 us -> 47.9 us (0.26)
  waiting for transfers between devices: 149 us -> 0 us
  Pallas kernels: 0 us -> 36.7 us
  between operations: 15.5 us -> 1.95 us
  local copies, waits for them, and re-layouts: 0.04 us -> 8.87 us
  starting transfers between devices: 7.61 us -> 0 us
  other arithmetic: 5.75 us -> 0 us
  matrix products: 5.68 us -> 0 us
    psum x1 -> x0, waiting for transfers between devices: 90.4 us -> none  [broadcast(): return lax.psum(kept, axis)]
    reduce_scatter x1 -> x0, waiting for transfers between devices: 58.4 us -> none  [on_device(): lax.psum_scatter(jnp.dot(spread, value_weight, preferred_element_type=jnp...]
    pallas_call x0 -> x1, Pallas kernels: none -> 36.7 us  [on_device(): pl.pallas_call(functools.partial(kernel, n), out_shape=(jax.ShapeDtypeStr...]
    unnamed x10 -> x18, local copies, waits for them, and re-layouts: 0.03 us -> 8.87 us
    all_to_all x1 -> x0, starting transfers between devices: 7.53 us -> none  [on_device(): lax.all_to_all(hidden_norm_rows, 'adapt', split_axis=1, concat_axis=0, ti...]
    dot_general x5 -> x0, matrix products: 5.68 us -> none  [the longest x1 2.45 us: on_device(): jnp.dot(reduced_rank_state, up_map, preferred_element_type=jnp.float32)]
    select_n x2 -> x0, other arithmetic: 3.91 us -> none  [broadcast(): jnp.where(lax.axis_index(axis) == source, value, 0).astype(value.dtype)]
  transfers between devices with their start and end apart: 3 -> 0, of which waited for: 3 -> 0; matrix products, arithmetic and copies ran while one was open for 4% -> 0% of each run, Pallas kernels for 0% -> 0%
where the time goes in v1:
time: 47.9 us; the launch traced here: 47.5 us
  Pallas kernels  36.7 us (77%)
  local copies, waits for them, and re-layouts  8.87 us (19%)
  between operations  1.95 us (4%)
    pallas_call x1, Pallas kernels, on_device(): pl.pallas_call(functools.partial(kernel, n), out_shape=(jax.ShapeDtypeStr...  36.7 us
    unnamed x18, local copies, waits for them, and re-layouts  8.87 us

profile of v1, /device:TPU:0, one launch (start us, length us, event | category | flops | bytes accessed | tf_op | source)
XLA Modules:
  0.0 47.5 jit_solution(8794212625430042369)
XLA Ops:
  1.9 0.0 copy-start
  1.9 1.2 %copy-done = bf16[512,1024]{1,0:T(8,128)(2,1)S(1)} copy-done((bf16[512,1024]{1,0:T(8,128)(2,1)S(1)}, bf16[512,1024]{1,0:T(8,128)(2,1)}, u32[]{:S(2)}) %copy-start) | copy-done | bytes 1048600
  3.1 0.0 copy-start.1
  3.2 1.1 %copy-done.1 = bf16[6,64,1024]{2,1,0:T(8,128)(2,1)S(1)} copy-done((bf16[6,64,1024]{2,1,0:T(8,128)(2,1)S(1)}, bf16[6,64,1024]{2,1,0:T(8,128)(2,1)}, u32[]{:S(2)}) %copy-start.1) | copy-done | bytes 786456
  4.3 0.0 copy-start.2
  4.3 1.0 %copy-done.2 = bf16[8,32,1024]{2,1,0:T(8,128)(2,1)S(1)} copy-done((bf16[8,32,1024]{2,1,0:T(8,128)(2,1)S(1)}, bf16[8,32,1024]{2,1,0:T(8,128)(2,1)}, u32[]{:S(2)}) %copy-start.2) | copy-done | bytes 524312
  5.3 0.0 copy-start.3
  5.3 1.0 %copy-done.3 = bf16[8,32,1024]{2,1,0:T(8,128)(2,1)S(1)} copy-done((bf16[8,32,1024]{2,1,0:T(8,128)(2,1)S(1)}, bf16[8,32,1024]{2,1,0:T(8,128)(2,1)}, u32[]{:S(2)}) %copy-start.3) | copy-done | bytes 524312
  6.4 0.0 copy-start.4
  6.4 0.9 %copy-done.4 = bf16[8,8192]{1,0:T(8,128)(2,1)S(1)} copy-done((bf16[8,8192]{1,0:T(8,128)(2,1)S(1)}, bf16[8,8192]{1,0:T(8,128)(2,1)}, u32[]{:S(2)}) %copy-start.4) | copy-done | bytes 131096
  7.3 0.0 copy-start.5
  7.3 0.9 %copy-done.5 = bf16[8,8192]{1,0:T(8,128)(2,1)S(1)} copy-done((bf16[8,8192]{1,0:T(8,128)(2,1)S(1)}, bf16[8,8192]{1,0:T(8,128)(2,1)}, u32[]{:S(2)}) %copy-start.5) | copy-done | bytes 131096
  8.2 0.0 copy-start.6
  8.2 0.7 %copy-done.6 = bf16[8,1024]{1,0:T(8,128)(2,1)S(1)} copy-done((bf16[8,1024]{1,0:T(8,128)(2,1)S(1)}, bf16[8,1024]{1,0:T(8,128)(2,1)}, u32[]{:S(2)}) %copy-start.6) | copy-done | bytes 16408
  8.9 0.0 copy-start.7
  8.9 0.7 %copy-done.7 = s32[8]{0:T(128)S(1)} copy-done((s32[8]{0:T(128)S(1)}, s32[8]{0:T(128)}, u32[]{:S(2)}) %copy-start.7) | copy-done | bytes 56
  9.6 36.7 %shard_map.122 = (bf16[8,1024]{1,0:T(8,128)(2,1)S(1)}, bf16[8,8192]{1,0:T(8,128)(2,1)S(1)}) custom-call(s32[1]{0:T(128)S(6)} %copy.15.adapter_ref, s32[1]{0:T(128)S(6)} %copy.16.live_ref, s32[8]{0:T(128)S(1)} %copy-done.7, bf16[8,8192]{1,0:T(8,128)(2,1)S(1)} %copy-done.4, bf16[512,1024]{1,0:T(8,128)(2,1)S(1)} %copy-done, bf16[6,64,8192]{2,1,0:T(8,128)(2,1)} %bitcast.1, ...), custom_call_target="tpu_custom_call" | custom-call | tf_op jit(solution)/shard_map/pallas_call | solution.py:287
  46.2 0.6 %copy.17 = bf16[8,1024]{1,0:T(8,128)(2,1)} copy(bf16[8,1024]{1,0:T(8,128)(2,1)S(1)} %get-tuple-element.4) | data formatting | bytes 32768
  46.8 0.7 %copy.18 = bf16[8,8192]{1,0:T(8,128)(2,1)} copy(bf16[8,8192]{1,0:T(8,128)(2,1)S(1)} %get-tuple-element.5) | data formatting | bytes 262144
Async XLA Ops:
  1.9 1.2 %copy-start = (bf16[512,1024]{1,0:T(8,128)(2,1)S(1)}, bf16[512,1024]{1,0:T(8,128)(2,1)}, u32[]{:S(2)}) copy-start(bf16[512,1024]{1,0:T(8,128)(2,1)} %weight_hbm.1) | copy-start | bytes 3145732
  3.1 1.1 %copy-start.1 = (bf16[6,64,1024]{2,1,0:T(8,128)(2,1)S(1)}, bf16[6,64,1024]{2,1,0:T(8,128)(2,1)}, u32[]{:S(2)}) copy-start(bf16[6,64,1024]{2,1,0:T(8,128)(2,1)} %up_hbm.1) | copy-start | bytes 2359300
  4.3 1.0 %copy-start.2 = (bf16[8,32,1024]{2,1,0:T(8,128)(2,1)S(1)}, bf16[8,32,1024]{2,1,0:T(8,128)(2,1)}, u32[]{:S(2)}) copy-start(bf16[8,32,1024]{2,1,0:T(8,128)(2,1)} %key_hbm.1) | copy-start | bytes 1572868
  5.3 1.0 %copy-start.3 = (bf16[8,32,1024]{2,1,0:T(8,128)(2,1)S(1)}, bf16[8,32,1024]{2,1,0:T(8,128)(2,1)}, u32[]{:S(2)}) copy-start(bf16[8,32,1024]{2,1,0:T(8,128)(2,1)} %value_hbm.1) | copy-start | bytes 1572868
  6.4 0.9 %copy-start.4 = (bf16[8,8192]{1,0:T(8,128)(2,1)S(1)}, bf16[8,8192]{1,0:T(8,128)(2,1)}, u32[]{:S(2)}) copy-start(bf16[8,8192]{1,0:T(8,128)(2,1)} %hidden_ref.1) | copy-start | bytes 393220
  7.3 0.9 %copy-start.5 = (bf16[8,8192]{1,0:T(8,128)(2,1)S(1)}, bf16[8,8192]{1,0:T(8,128)(2,1)}, u32[]{:S(2)}) copy-start(bf16[8,8192]{1,0:T(8,128)(2,1)} %query_hbm.1) | copy-start | bytes 393220
  8.2 0.7 %copy-start.6 = (bf16[8,1024]{1,0:T(8,128)(2,1)S(1)}, bf16[8,1024]{1,0:T(8,128)(2,1)}, u32[]{:S(2)}) copy-start(bf16[8,1024]{1,0:T(8,128)(2,1)} %fresh_hbm.1) | copy-start | bytes 49156
  8.9 0.7 %copy-start.7 = (s32[8]{0:T(128)S(1)}, s32[8]{0:T(128)}, u32[]{:S(2)}) copy-start(s32[8]{0:T(128)} %length_ref.1) | copy-start | bytes 100

commit v2 on v1

--- a/solution.py
+++ b/solution.py
@@ -21,7 +21,7 @@
     adapter_ref,
     live_ref,
     length_ref,
-    hidden_ref,
+    hidden_hbm,
     weight_hbm,
     down_hbm,
     up_hbm,
@@ -31,6 +31,8 @@
     value_hbm,
     new_value_ref,
     attended_ref,
+    hidden_v,
+    quarters,
     gathered,
     plane_rows,
     partial,
@@ -38,6 +40,12 @@
     weight_v,
     down_v,
     up_v,
+    down_own,
+    down_chip,
+    down_plane,
+    up_own,
+    up_chip,
+    up_plane,
     query_v,
     fresh_v,
     key_v,
@@ -46,35 +54,41 @@
     fresh_weight_v,
     local_sem,
     send_sem,
-    recv_sem,
+    mate_sem,
+    gather_sem,
+    pair_sem,
     sum_send_sem,
     sum_recv_sem,
 ):
-    rows = hidden_ref.shape[0]
+    rows = hidden_v.shape[0]
     features = weight_v.shape[0]
     resident = down_v.shape[0]
     cached = key_v.shape[1]
+    blocks = down_own.shape[1]
+    half = up_own.shape[3]
     planes = n // PLANE
     me = lax.axis_index("adapt")
     core = lax.rem(me, 2)
     column = lax.rem(lax.div(me, 2), 2)
     level = lax.div(me, PLANE)
-
-    def at(z, y, c):
-        return z * PLANE + y * 2 + c
+    mine = column * 2 + core
+    f32, bf16 = jnp.float32, jnp.bfloat16
+
+    def at(z, q):
+        return z * PLANE + q
 
     locals_ = [
         pltpu.make_async_copy(src, dst, local_sem.at[i])
         for i, (src, dst) in enumerate(
             [
+                (hidden_hbm, hidden_v),
+                (down_hbm, down_v),
+                (up_hbm, up_v),
                 (query_hbm, query_v),
                 (fresh_hbm, fresh_v),
                 (key_hbm, key_v),
                 (value_hbm, value_v),
-                (hidden_ref, gathered.at[me]),
                 (weight_hbm, weight_v),
-                (up_hbm, up_v),
-                (down_hbm, down_v),
             ]
         )
     ]
@@ -89,38 +103,82 @@
             device_id={"adapt": lax.rem(me + k, n)},
             device_id_type=pl.DeviceIdType.MESH,
         )
+
+    locals_[0].wait()
+    for q in range(PLANE):
+        for z in range(planes):
+            first = (z * PLANE + q) * features
+            quarters[q, :, z * features : (z + 1) * features] = hidden_v[
+                :, first : first + features
+            ]
+    gathered[level, mine] = quarters[mine]
     pl.semaphore_wait(barrier, n - 1)
 
     sends = []
 
-    def give(block, target, own=False):
-        copy = pltpu.make_async_remote_copy(
-            src_ref=hidden_ref if own else gathered.at[block],
-            dst_ref=gathered.at[block],
-            send_sem=send_sem.at[len(sends)],
-            recv_sem=recv_sem.at[block],
+    def remote(src, dst, recv, target):
+        return pltpu.make_async_remote_copy(
+            src_ref=src,
+            dst_ref=dst,
+            send_sem=send_sem.at[min(len(sends), send_sem.shape[0] - 1)],
+            recv_sem=recv,
             device_id={"adapt": target},
             device_id_type=pl.DeviceIdType.MESH,
         )
+
+    def give(src, dst, recv, target):
+        copy = remote(src, dst, recv, target)
         copy.start()
         sends.append(copy)
 
-    def take(block):
-        pltpu.make_async_remote_copy(
-            src_ref=gathered.at[block],
-            dst_ref=gathered.at[block],
-            send_sem=send_sem.at[0],
-            recv_sem=recv_sem.at[block],
-            device_id={"adapt": at(level, column, 1 - core)},
-            device_id_type=pl.DeviceIdType.MESH,
-        ).wait_recv()
-
-    sibling = at(level, column, 1 - core)
-    across = at(level, 1 - column, core)
-    give(me, across, own=True)
+    sibling_place = column * 2 + 1 - core
+    across_place = (1 - column) * 2 + core
+    corner_place = (1 - column) * 2 + 1 - core
+    mates = (across_place, corner_place, sibling_place)
+    sibling, across = at(level, sibling_place), at(level, across_place)
+    for q in mates:
+        give(quarters.at[q], gathered.at[level, mine], mate_sem.at[mine], at(level, q))
+
+    def take(ref, recv):
+        remote(ref, ref, recv, sibling).wait_recv()
+
+    locals_[1].wait()
+    locals_[2].wait()
+    for b in range(blocks):
+        wanted = adapter_ref[b] - me * resident
+        held = (wanted >= 0) & (wanted < resident)
+        wanted = jnp.clip(wanted, 0, resident - 1)
+        keep = jnp.where(held, 1.0, 0.0).astype(bf16)
+        for q in range(PLANE):
+            for z in range(planes):
+                first = (z * PLANE + q) * features
+                down_own[q, b, :, z * features : (z + 1) * features] = (
+                    down_v[wanted, :, first : first + features] * keep
+                )
+        for c in range(2):
+            up_own[c, b] = up_v[wanted, :, c * half : (c + 1) * half] * keep
+    give(down_own.at[corner_place], down_chip.at[1 - column], pair_sem.at[0], sibling)
+    give(down_own.at[sibling_place], down_chip.at[column], pair_sem.at[1], sibling)
+    give(up_own, up_chip, pair_sem.at[2], sibling)
+
+    for q in mates:
+        take(gathered.at[level, q], mate_sem.at[q])
     for k in range(1, planes):
-        give(me, at(lax.rem(level + k, planes), column, core), own=True)
-    give(me, sibling, own=True)
+        give(
+            gathered.at[level],
+            gathered.at[level],
+            gather_sem.at[level],
+            at(lax.rem(level + k, planes), mine),
+        )
+
+    take(down_chip.at[1 - column], pair_sem.at[0])
+    down_own[across_place] = down_own[across_place] + down_chip[1 - column]
+    give(down_own.at[across_place], down_plane, pair_sem.at[3], across)
+    take(up_chip, pair_sem.at[2])
+    for c in range(2):
+        up_chip[c] = up_chip[c] + up_own[c]
+    give(up_chip.at[core], up_plane.at[core], pair_sem.at[4], across)
+    up_sent = sends[-1]
 
     sequence = lax.broadcasted_iota(jnp.int32, (rows * GROUP, 1), 0)
     row_of = lax.rem(sequence, rows)
@@ -164,31 +222,26 @@
 
     def process(k):
         z = lax.rem(level + planes - k, planes)
-        for y, c in ((column, 1 - core), (1 - column, 1 - core)):
-            take(at(z, y, c))
+        if k:
+            take(gathered.at[z], gather_sem.at[z])
         plane_rows[...] = jnp.concatenate(
-            [gathered[z * PLANE + i].astype(jnp.float32) for i in range(PLANE)], axis=0
-        ).astype(jnp.bfloat16)
-        wanted = adapter_ref[lax.div(z * PLANE * rows, BLOCK_ROWS)] - me * resident
-        held = (wanted >= 0) & (wanted < resident)
-        wanted = jnp.clip(wanted, 0, resident - 1)
+            [gathered[z, q].astype(f32) for q in range(PLANE)], axis=0
+        ).astype(bf16)
+        block = lax.div(z * PLANE * rows, BLOCK_ROWS)
         state = lax.dot_general(
-            plane_rows[...], down_v[wanted], NT, preferred_element_type=jnp.float32
-        )
-        columns = pl.ds(pl.multiple_of(me * features, features), features)
-        base = jnp.dot(
-            plane_rows[:, columns], weight_v[...], preferred_element_type=jnp.float32
-        )
-        delta = jnp.dot(
-            state.astype(jnp.bfloat16), up_v[wanted], preferred_element_type=jnp.float32
-        )
-        share = base + jnp.where(held, delta, 0.0)
-        for i in range(PLANE):
-            partial[z * PLANE + i] = share[i * rows : (i + 1) * rows].astype(jnp.bfloat16)
-        targets = [at(z, y, c) for y in (1 - column, column) for c in (core, 1 - core)]
-        if k == 0:
-            targets = [at(z, 1 - column, core), at(z, 1 - column, 1 - core), sibling]
-        for target in targets:
+            plane_rows[...], down_own[mine, block], NT, preferred_element_type=f32
+        ).astype(bf16)
+        columns = pl.ds(pl.multiple_of(level * features, features), features)
+        base = jnp.dot(plane_rows[:, columns], weight_v[...], preferred_element_type=f32)
+        for c in range(2):
+            lanes = slice(c * half, (c + 1) * half)
+            share = base[:, lanes] + jnp.dot(
+                state, up_chip[c, block], preferred_element_type=f32
+            )
+            for q in range(PLANE):
+                partial[z * PLANE + q, :, lanes] = share[q * rows : (q + 1) * rows].astype(bf16)
+        for q in mates if k == 0 else mates + (mine,):
+            target = at(z, q)
             copy = pltpu.make_async_remote_copy(
                 src_ref=partial.at[target],
                 dst_ref=landed.at[me],
@@ -200,37 +253,23 @@
             copy.start()
             sum_sends.append(copy)
 
-    for copy in locals_[:4]:
+    for copy in locals_[3:]:
         copy.wait()
-    attend(0)
-    attend(1)
-    take(across)
-    give(across, sibling)
-    attend(2)
-    attend(3)
-    for copy in locals_[4:]:
-        copy.wait()
-    todo = list(range(4, KV_HEADS))
-    for k in range(1, planes):
-        z = lax.rem(level + planes - k, planes)
-        block = at(z, column, core)
-        take(block)
-        give(block, across)
-        give(block, sibling)
-        if k >= 2:
-            before = at(lax.rem(level + planes - (k - 1), planes), 1 - column, core)
-            take(before)
-            give(before, sibling)
-        process(k - 1)
-        if todo:
-            attend(todo.pop(0))
-    last = at(lax.rem(level + 1, planes), 1 - column, core)
-    if planes > 1:
-        take(last)
-        give(last, sibling)
-    while todo:
-        attend(todo.pop(0))
-    process(planes - 1)
+    for g in range(KV_HEADS // 2):
+        attend(g)
+    take(up_plane.at[core], pair_sem.at[4])
+    give(up_plane.at[core], up_plane.at[core], pair_sem.at[5], sibling)
+    for g in range(KV_HEADS // 2, KV_HEADS):
+        attend(g)
+    take(down_chip.at[column], pair_sem.at[1])
+    take(down_plane, pair_sem.at[3])
+    down_own[mine] = down_own[mine] + down_chip[column] + down_plane[...]
+    take(up_plane.at[1 - core], pair_sem.at[5])
+    up_sent.wait_send()
+    for c in range(2):
+        up_chip[c] = up_chip[c] + up_plane[c]
+    for k in range(planes):
+        process(k)
 
     total = partial[me].astype(jnp.float32)
     for k in range(1, n):
@@ -258,7 +297,8 @@
             head = g * GROUP + h
             attended_ref[:, head * HD : (head + 1) * HD] = (live * mixed).astype(jnp.bfloat16)
     for copy in sends + sum_sends:
-        copy.wait_send()
+        if copy is not up_sent:
+            copy.wait_send()
 
 
 def on_device(
@@ -280,7 +320,9 @@
     wide = value_weight.shape[1]
     planes = n // PLANE
     bf16 = jnp.bfloat16
-    sends = 3 * (planes - 1) + 2 + planes
+    blocks = adapter_per_block.shape[0]
+    sends = 3 + 3 + (planes - 1) + 2 + 1
+    rank, quarter, half = down.shape[1], width // PLANE, wide // 2
     smem = pl.BlockSpec(memory_space=pltpu.SMEM)
     anywhere = pl.BlockSpec(memory_space=pl.ANY)
     vmem = pl.BlockSpec(memory_space=pltpu.VMEM)
@@ -293,13 +335,21 @@
         in_specs=[smem] * 3 + [anywhere] * 8,
         out_specs=(vmem, vmem),
         scratch_shapes=[
-            pltpu.VMEM((n, rows, width), bf16),
-            pltpu.VMEM((PLANE * rows, width), bf16),
+            pltpu.VMEM((rows, width), bf16),
+            pltpu.VMEM((PLANE, rows, quarter), bf16),
+            pltpu.VMEM((planes, PLANE, rows, quarter), bf16),
+            pltpu.VMEM((PLANE * rows, quarter), bf16),
             pltpu.VMEM((n, rows, wide), bf16),
             pltpu.VMEM((n, rows, wide), bf16),
             pltpu.VMEM(value_weight.shape, bf16),
             pltpu.VMEM(down.shape, bf16),
             pltpu.VMEM(adapter_up_weight.shape, bf16),
+            pltpu.VMEM((PLANE, blocks, rank, quarter), bf16),
+            pltpu.VMEM((2, blocks, rank, quarter), bf16),
+            pltpu.VMEM((blocks, rank, quarter), bf16),
+            pltpu.VMEM((2, blocks, rank, half), bf16),
+            pltpu.VMEM((2, blocks, rank, half), bf16),
+            pltpu.VMEM((2, blocks, rank, half), bf16),
             pltpu.VMEM(queries.shape, bf16),
             pltpu.VMEM(incoming_key.shape, bf16),
             pltpu.VMEM(key_cache.shape, bf16),
@@ -308,12 +358,14 @@
             pltpu.VMEM((KV_HEADS, GROUP * rows, HD), jnp.float32),
             pltpu.SemaphoreType.DMA((8,)),
             pltpu.SemaphoreType.DMA((sends,)),
-            pltpu.SemaphoreType.DMA((n,)),
+            pltpu.SemaphoreType.DMA((PLANE,)),
+            pltpu.SemaphoreType.DMA((planes,)),
+            pltpu.SemaphoreType.DMA((6,)),
             pltpu.SemaphoreType.DMA((n,)),
             pltpu.SemaphoreType.DMA((n,)),
         ],
         compiler_params=pltpu.CompilerParams(
-            collective_id=0, has_side_effects=True, vmem_limit_bytes=48 * 1024 * 1024
+            collective_id=0, has_side_effects=True, vmem_limit_bytes=63 * 1024 * 1024
         ),
     )(
         adapter_per_block,

time: 47.9 us -> 35.1 us (0.73)
  Pallas kernels: 36.7 us -> 30 us
  local copies, waits for them, and re-layouts: 8.87 us -> 2.89 us
    pallas_call x1, Pallas kernels: 36.7 us -> 30 us  [on_device(): pl.pallas_call(functools.partial(kernel, n), out_shape=(jax.ShapeDtypeStr...]
    unnamed x18 -> x2, local copies, waits for them, and re-layouts: 8.87 us -> 2.89 us
where the time goes in v2:
time: 35.1 us; the launch traced here: 34.8 us
  Pallas kernels  30 us (85%)
  local copies, waits for them, and re-layouts  2.89 us (8%)
  between operations  1.93 us (5%)
    pallas_call x1, Pallas kernels, on_device(): pl.pallas_call(functools.partial(kernel, n), out_shape=(jax.ShapeDtypeStr...  30 us
    unnamed x2, local copies, waits for them, and re-layouts  2.89 us

profile of v2, /device:TPU:0, one launch (start us, length us, event | category | flops | bytes accessed | tf_op | source)
XLA Modules:
  0.0 34.8 jit_solution(8452941756549186217)
XLA Ops:
  1.9 30.0 %shard_map.122 = (bf16[8,1024]{1,0:T(8,128)(2,1)}, bf16[8,8192]{1,0:T(8,128)(2,1)}) custom-call(s32[1]{0:T(128)S(6)} %copy.15.adapter_ref, s32[1]{0:T(128)S(6)} %copy.16.live_ref, s32[8]{0:T(128)} %length_ref.1, bf16[8,8192]{1,0:T(8,128)(2,1)} %hidden_hbm.1, bf16[512,1024]{1,0:T(8,128)(2,1)} %weight_hbm.1, bf16[6,64,8192]{2,1,0:T(8,128)(2,1)} %bitcast.1, ...), custom_call_target="tpu_custom_call" | custom-call | tf_op jit(solution)/shard_map/pallas_call | solution.py:329
  31.9 1.3 %copy.17 = bf16[8,1024]{1,0:T(8,128)(2,1)} copy(bf16[8,1024]{1,0:T(8,128)(2,1)} %get-tuple-element.4) | data formatting | bytes 32768
  33.3 1.6 %copy.18 = bf16[8,8192]{1,0:T(8,128)(2,1)} copy(bf16[8,8192]{1,0:T(8,128)(2,1)} %get-tuple-element.5) | data formatting | bytes 262144
